TPU v7x, 256 devices: a whole 4x4x8 slice. The times are simulated.
256 devices in a mesh: grp: 8 (over x, z_hi), seq: 32 (over z_lo, y, core).
Axes of the slice: x: 4, y: 4, z: 8 (z_hi: 2, z_lo: 4; z = z_hi * 4 + z_lo), core: 2. Of those that a mesh axis runs over, the one named last changes fastest.
Arguments:
- rows_alpha: bfloat16 [3, 8192, 8192], P(None, 'grp', 'seq'), may hold values from -40 to 40
- rows_beta: bfloat16 [3, 8192, 8192], P(None, 'grp', 'seq'), may hold values from -40 to 40
- filter_alpha: float32 [8192, 128], P(('grp', 'seq')), may hold values from -1 to 1
- filter_beta: float32 [8192, 128], P(('grp', 'seq')), may hold values from -1 to 1
Outputs:
- correlation: float32 [8192, 8192], P(('grp', 'seq'))
All inputs are finite; a program needn't handle non-finite values.
Results may differ from a plain program's by a relative error of at most 0.0038.
Values may be sent and summed in bfloat16 or wider, within the bound.
A program may use at most 128 MiB of HBM per device.

v0:
```python
import jax
import jax.numpy as jnp
import numpy as np
from jax import lax
from jax.sharding import PartitionSpec as P


def toeplitz_pair(filter_taps):
    width = filter_taps.shape[1]
    row_index = np.arange(width)[:, None]
    col_index = np.arange(width)[None, :]
    tap_index = jnp.asarray((row_index - col_index) % width, dtype=jnp.int32)
    circulant = filter_taps[:, tap_index]
    lower = jnp.asarray(row_index - col_index >= 0)
    near_part = jnp.where(lower[None], circulant, jnp.float32(0.0))
    far_part = jnp.where(lower[None], jnp.float32(0.0), circulant)
    return (near_part, far_part)


def mix_conv(rows, filter_taps):
    channels = rows.shape[1]
    length_all = rows.shape[2]
    width = filter_taps.shape[1]
    query_part = rows[0].astype(jnp.float32)
    product = rows[1].astype(jnp.float32) * rows[2].astype(jnp.float32)
    blocks = product.reshape(channels, length_all // width, width)
    previous = jnp.pad(blocks, ((0, 0), (1, 0), (0, 0)))[:, :-1]
    near_part, far_part = toeplitz_pair(filter_taps)
    convolved = jnp.einsum("cab,cjb->cja", near_part, blocks, precision=lax.Precision.HIGHEST)
    convolved = convolved + jnp.einsum(
        "cab,cjb->cja", far_part, previous, precision=lax.Precision.HIGHEST
    )
    gated_out = query_part * convolved.reshape(channels, length_all)
    average = jnp.mean(gated_out, axis=1, keepdims=True)
    centred = gated_out - average
    variance = jnp.mean(centred * centred, axis=1, keepdims=True)
    return (centred * lax.rsqrt(variance + 1e-05)).astype(jnp.bfloat16)


def body(rows_alpha, rows_beta, filter_alpha, filter_beta):
    owned_alpha = lax.all_to_all(rows_alpha, "seq", split_axis=1, concat_axis=2, tiled=True)
    owned_beta = lax.all_to_all(rows_beta, "seq", split_axis=1, concat_axis=2, tiled=True)
    normed_alpha = mix_conv(owned_alpha, filter_alpha)
    normed_beta = mix_conv(owned_beta, filter_beta)
    panel_alpha, panel_beta = (
        lax.all_to_all(normed_alpha, "seq", split_axis=1, concat_axis=0, tiled=True),
        lax.all_to_all(normed_beta, "seq", split_axis=1, concat_axis=0, tiled=True),
    )
    inverse_count = 1.0 / (panel_alpha.shape[1] * lax.axis_size("seq"))
    gathered = lax.all_gather(panel_beta, "grp", axis=0, tiled=True)
    product = lax.dot_general(
        panel_alpha, gathered, (((1,), (1,)), ((), ())), preferred_element_type=jnp.float32
    )
    return lax.psum_scatter(product * inverse_count, "seq", scatter_dimension=0, tiled=True)


def solution(mesh):
    placed = (
        P(None, "grp", "seq"),
        P(None, "grp", "seq"),
        P(("grp", "seq"), None),
        P(("grp", "seq"), None),
    )
    return jax.shard_map(
        body, mesh=mesh, in_specs=placed, out_specs=P(("grp", "seq"), None), check_vma=False
    )
```

profile of v0, /device:TPU:4, one launch (start us, length us, event | category | flops | bytes accessed | tf_op | source)
XLA Modules:
  0.0 512.7 jit_solution(7462403061441688750)
XLA Ops:
  6.5 4.1 copy.37
  10.6 9.2 %all-to-all-start.2 = ((bf16[3,1024,256]{2,0,1:T(4,128)(2,1)}), bf16[3,1024,256]{2,0,1:T(4,128)(2,1)}, u32[]{:S(2)}, u32[]{:S(2)}) async-start(bf16[3,1024,256]{2,0,1:T(4,128)(2,1)} %copy.37), calls=%async_computation.2 | async-start | bytes 4194304 | tf_op jit(solution)/shard_map/all_to_all | solution.py:42
  20.0 54.4 %gather_fusion.1 = f32[16384,32]{1,0:T(8,128)} fusion(f32[32,128]{0,1:T(8,128)S(1)} %copy.40, s32[16384]{0:T(1024)S(1)} %broadcast_clamp_fusion), kind=kCustom, calls=%fused_computation.1 | custom fusion | bytes 4259840 | tf_op jit(solution)/shard_map/gather | solution.py:13
  74.4 5.5 %copy.41 = f32[128,128,32]{1,0,2:T(8,128)S(1)} copy(f32[128,128,32]{2,1,0:T(8,128)} %bitcast.67) | data formatting | bytes 4194304 | tf_op jit(solution)/shard_map/gather | solution.py:13
  80.0 1.8 copy.38
  86.2 2.8 copy.44
  89.0 2.3 reshape.113
  91.2 4.2 fusion
  95.5 5.2 %fusion.36 = (f32[32]{0:T(128)S(1)}, f32[32,64,128]{2,1,0:T(8,128)S(1)}, f32[32,64,128]{2,1,0:T(8,128)}) fusion(f32[32,64,128]{2,1,0:T(8,128)S(1)} %copy-done.4, f32[32,64,128]{2,1,0:T(8,128)S(1)} %fusion, f32[32,64,128]{2,1,0:T(8,128)S(1)} %mul.70, f32[128,128,32]{1,0,2:T(8,128)S(1)} %copy.41, pred[128,128]{1,0:T(8,128)(4,1)S(1)} %bitcast.77), kind=kOutput, calls=%fused_computation.50 | convolution fusion | flops 403963872 | bytes 7356544 | tf_op jit(solution)/shard_map/cab,cjb->cja/dot_general | solution.py:29
  102.8 1.8 fusion.20
  104.6 23.4 %all_to_all.62 = bf16[32,32,256]{2,0,1:T(8,128)(2,1)} all-to-all(bf16[32,32,256]{2,0,1:T(8,128)(2,1)S(1)} %fusion.20), channel_id=1, replica_groups=mesh['grp'=8,'seq'=32] {'seq'}, dimensions={1} | all-to-all | bytes 1048576 | tf_op jit(solution)/shard_map/all_to_all | solution.py:47
  128.0 2.7 copy.29
  130.7 4.9 all-to-all-start
  135.8 54.4 %gather_fusion = f32[16384,32]{1,0:T(8,128)} fusion(f32[32,128]{0,1:T(8,128)S(1)} %copy.32, s32[16384]{0:T(1024)S(1)} %broadcast_clamp_fusion), kind=kCustom, calls=%fused_computation | custom fusion | bytes 4259840 | tf_op jit(solution)/shard_map/gather | solution.py:13
  190.2 5.5 %copy.33 = f32[128,128,32]{1,0,2:T(8,128)S(1)} copy(f32[128,128,32]{2,1,0:T(8,128)} %bitcast.66) | data formatting | bytes 4194304 | tf_op jit(solution)/shard_map/gather | solution.py:13
  195.8 44.8 %all-to-all-done = bf16[3,1024,256]{2,0,1:T(4,128)(2,1)} async-done(((bf16[3,1024,256]{2,0,1:T(4,128)(2,1)}), bf16[3,1024,256]{2,0,1:T(4,128)(2,1)}, u32[]{:S(2)}, u32[]{:S(2)}) %all-to-all-start) | async-done | bytes 1572896 | tf_op jit(solution)/shard_map/all_to_all | solution.py:41
  240.5 1.8 copy.30
  249.1 2.3 reshape.111
  251.4 4.2 fusion.4
  255.6 5.5 %fusion.37 = (f32[32]{0:T(128)S(1)}, f32[32,64,128]{2,1,0:T(8,128)}, f32[32,64,128]{2,1,0:T(8,128)}) fusion(f32[32,64,128]{2,1,0:T(8,128)S(1)} %copy-done.3, f32[32,64,128]{2,1,0:T(8,128)S(1)} %fusion.4, f32[32,64,128]{2,1,0:T(8,128)S(1)} %mul.63, f32[128,128,32]{1,0,2:T(8,128)S(1)} %copy.33, pred[128,128]{1,0:T(8,128)(4,1)S(1)} %bitcast.79), kind=kOutput, calls=%fused_computation.51 | convolution fusion | flops 403963872 | bytes 7356544 | tf_op jit(solution)/shard_map/cab,cjb->cja/dot_general | solution.py:29
  263.3 1.7 fusion.23
  265.0 21.2 %all_to_all.63 = bf16[32,32,256]{2,0,1:T(8,128)(2,1)S(1)} all-to-all(bf16[32,32,256]{2,0,1:T(8,128)(2,1)S(1)} %fusion.23), channel_id=1, replica_groups=mesh['grp'=8,'seq'=32] {'seq'}, dimensions={1} | all-to-all | bytes 1048576 | tf_op jit(solution)/shard_map/all_to_all | solution.py:46
  286.3 15.3 %convolution_multiply_fusion = f32[1024,8192]{1,0:T(8,128)} fusion(bf16[1024,256]{1,0:T(8,128)(2,1)S(1)} %bitcast.74, bf16[8192,256]{1,0:T(8,128)(2,1)} %all-gather.2.cloned.1.call-done), kind=kOutput, calls=%fused_computation.2 | convolution fusion | flops 4303355904 | bytes 38273024 | tf_op jit(solution)/shard_map/dot_general | solution.py:51
  301.6 204.3 %reduce-scatter.2.cloned.1.call-done = f32[32,8192]{1,0:T(8,128)} async-done(((f32[1024,8192]{1,0:T(8,128)}), f32[32,8192]{1,0:T(8,128)}) %reduce-scatter.2.cloned.1.call-update) | async-done | bytes 1048592 | tf_op jit(solution)/shard_map/reduce_scatter | solution.py:54
  (46 shorter events, 15.7 us)
Async XLA Ops:
  10.6 9.2 %copy-start.8 = (f32[32,128]{1,0:T(8,128)S(1)}, f32[32,128]{1,0:T(8,128)}, u32[]{:S(2)}) copy-start(f32[32,128]{1,0:T(8,128)} %param.11) | copy-start | bytes 49156
  10.6 9.4 %copy-start.7 = (s32[16384]{0:T(1024)S(1)}, s32[16384]{0:T(1024)}, u32[]{:S(2)}) copy-start(s32[16384]{0:T(1024)} %constant.33) | copy-start | bytes 196612
  10.6 69.3 %all-to-all-start.2 = ((bf16[3,1024,256]{2,0,1:T(4,128)(2,1)}), bf16[3,1024,256]{2,0,1:T(4,128)(2,1)}, u32[]{:S(2)}, u32[]{:S(2)}) async-start(bf16[3,1024,256]{2,0,1:T(4,128)(2,1)} %copy.37), calls=%async_computation.2 | async-start | bytes 4194304 | tf_op jit(solution)/shard_map/all_to_all | solution.py:42
  19.8 266.5 %all-gather.2.cloned.1.call-start = ((), (), s32[]{:S(2)}) async-start(), calls=%async_computation.5 | async-start | bytes 4718592 | tf_op jit(solution)/shard_map/all_gather | solution.py:50
  81.8 1.5 copy-start.1
  86.1 5.1 copy-start.6
  91.2 4.2 copy-start.4
  102.7 25.3 %copy-start.5 = (bf16[3,1024,256]{2,1,0:T(8,128)(2,1)S(1)}, bf16[3,1024,256]{2,1,0:T(8,128)(2,1)}, u32[]{:S(2)}) copy-start(bf16[3,1024,256]{2,1,0:T(8,128)(2,1)} %param.8) | copy-start | bytes 4718596
  130.7 5.0 copy-start.9
  130.7 109.8 %all-to-all-start = ((bf16[3,1024,256]{2,0,1:T(4,128)(2,1)}), bf16[3,1024,256]{2,0,1:T(4,128)(2,1)}, u32[]{:S(2)}, u32[]{:S(2)}) async-start(bf16[3,1024,256]{2,0,1:T(4,128)(2,1)} %copy.29), calls=%async_computation | async-start | bytes 4194304 | tf_op jit(solution)/shard_map/all_to_all | solution.py:41
  135.7 370.2 %reduce-scatter.2.cloned.1.call-start = ((), (), s32[]{:S(2)}) async-start(), calls=%async_computation.6 | async-start | bytes 34603008 | tf_op jit(solution)/shard_map/reduce_scatter | solution.py:54
  242.4 1.1 copy-start
  251.4 4.2 copy-start.3
  261.2 1.6 copy-start.2
Sparse Core Ops, SparseCore 0:
  128.1 98.7 all-gather.1
  301.7 204.1 reduce-scatter.1
where the time goes:
time: 514 us; the launch traced here: 513 us
  waiting for transfers between devices  249 us (48%)
  local copies, waits for them, and re-layouts  149 us (29%)
  blocking collectives  44.7 us (9%)
  matrix products  34.5 us (7%)
  starting transfers between devices  14.2 us (3%)
  between operations  13.6 us (3%)
  other arithmetic  7.36 us (1%)
    reduce_scatter x1, waiting for transfers between devices, body(): lax.psum_scatter(product * inverse_count, 'seq', scatter_dimension=0, til...  204 us
    gather x4, local copies, waits for them, and re-layouts, toeplitz_pair(): circulant = filter_taps[:, tap_index]  120 us
    all_to_all x1, waiting for transfers between devices, body(): lax.all_to_all(rows_alpha, 'seq', split_axis=1, concat_axis=2, tiled=True)  44.8 us
    all_to_all x1, blocking collectives, body(): lax.all_to_all(normed_beta, 'seq', split_axis=1, concat_axis=0, tiled=True)  23.4 us
    all_to_all x1, blocking collectives, body(): lax.all_to_all(normed_alpha, 'seq', split_axis=1, concat_axis=0, tiled=True)  21.2 us
    dot_general x1, matrix products, body(): lax.dot_general(panel_alpha, gathered, (((1,), (1,)), ((), ())), preferre...  15.3 us
    dot_general x2, matrix products, mix_conv(): jnp.einsum('cab,cjb->cja', near_part, blocks, precision=lax.Precision.HIG...  10.8 us
  transfers between devices with their start and end apart: 4, of which 2 were waited for; matrix products, arithmetic and copies ran while one was open for 29% of the time, Pallas kernels for 0%

commit v1 on v0

v1 whole, which is shorter than its diff:
```python
import functools

import jax
import jax.numpy as jnp
import ml_dtypes
import numpy as np
from jax import lax
from jax.experimental import pallas as pl
from jax.experimental.pallas import tpu as pltpu
from jax.sharding import PartitionSpec as P

MESH = pl.DeviceIdType.MESH
BF = jnp.bfloat16
F32 = jnp.float32
TOKENS = 8192
CHAN = 1024
TOK = 256
TAPS = 128
CHUNK = 256


def split_const(matrix):
    high = matrix.astype(ml_dtypes.bfloat16)
    low = (matrix - high.astype(np.float64)).astype(ml_dtypes.bfloat16)
    return high, low


def dft_constants():
    n = np.arange(256)[:, None]
    k = np.arange(128)[None, :] + 0.5
    angle = 2.0 * np.pi * n * k / 256.0
    forward = np.concatenate([np.cos(angle), -np.sin(angle)], axis=1)
    back = angle[128:].T
    inverse = np.concatenate([np.cos(back), -np.sin(back)], axis=0) / 128.0
    return split_const(forward) + split_const(inverse)


def split(value):
    high = value.astype(BF)
    low = (value - high.astype(F32)).astype(BF)
    return high, low


def dot3(value, w_high, w_low):
    high, low = split(value)
    total = jnp.dot(low, w_high, preferred_element_type=F32)
    total = total + jnp.dot(high, w_low, preferred_element_type=F32)
    return total + jnp.dot(high, w_high, preferred_element_type=F32)


def place():
    g = lax.axis_index("grp")
    s = lax.axis_index("seq")
    return g, s, g // 2, g % 2, s // 8, (s // 2) % 4, s % 2


def eye_mask():
    r = lax.broadcasted_iota(jnp.int32, (128, 128), 0)
    c = lax.broadcasted_iota(jnp.int32, (128, 128), 1)
    return r == c


def to_row(column, eye):
    return jnp.sum(jnp.where(eye, jnp.broadcast_to(column, (128, 128)), 0.0), axis=0, keepdims=True)


def to_column(row, eye):
    return jnp.sum(jnp.where(eye, jnp.broadcast_to(row, (128, 128)), 0.0), axis=1, keepdims=True)


def front_kernel(
    rows_a, rows_b, filt_a, filt_b, wf_hi, wf_lo, wi_hi, wi_lo, z_a, z_b,
    halo, taps, centred, own, level1, level2,
    h_send, h_recv, f1_send, f1_recv, f2_send, f2_recv, f3_send, f3_recv, s1_send, s1_recv, s2_send, s2_recv,
):
    g, s, _, _, zl, y, c = place()
    following = lax.rem(s + 1, 32)
    barrier = pltpu.get_barrier_semaphore()
    zl_peers = [lax.rem(zl + i, 4) for i in range(1, 4)]
    y_peers = [lax.rem(y + i, 4) for i in range(1, 4)]
    seq = lambda a, b, d: (g, a * 8 + b * 2 + d)
    pl.semaphore_signal(barrier, inc=1, device_id=(g, lax.rem(s + 31, 32)), device_id_type=MESH)
    for p in zl_peers:
        pl.semaphore_signal(barrier, inc=1, device_id=seq(p, y, c), device_id_type=MESH)
    for i in range(1, 8):
        q = lax.rem(y * 2 + c + i, 8)
        pl.semaphore_signal(barrier, inc=1, device_id=(g, zl * 8 + q), device_id_type=MESH)
    taps[c, y, zl, 0] = filt_a[...]
    taps[c, y, zl, 1] = filt_b[...]
    pl.semaphore_wait(barrier, 11)

    def copy(src, dst, send, recv, device):
        cp = pltpu.make_async_remote_copy(
            src_ref=src, dst_ref=dst, send_sem=send, recv_sem=recv, device_id=device, device_id_type=MESH
        )
        return cp

    sends = []

    def go(*args):
        cp = copy(*args)
        cp.start()
        sends.append(cp)

    for i, p in enumerate(zl_peers):
        mine = taps.at[c, y, zl]
        go(mine, mine, f1_send.at[i], f1_recv.at[zl], seq(p, y, c))
    for k, rows in enumerate((rows_b, rows_a)):
        go(rows.at[1:3, :, 128:256], halo.at[k], h_send.at[k], h_recv.at[k], (g, following))
    for p in zl_peers:
        got = taps.at[c, y, p]
        copy(got, got, f1_send.at[0], f1_recv.at[p], seq(p, y, c)).wait_recv()
    for i, p in enumerate(y_peers):
        mine = taps.at[c, y]
        go(mine, mine, f2_send.at[i], f2_recv.at[y], seq(zl, p, c))
    for p in y_peers:
        got = taps.at[c, p]
        copy(got, got, f2_send.at[0], f2_recv.at[p], seq(zl, p, c)).wait_recv()
    mine = taps.at[c]
    go(mine, mine, f3_send, f3_recv, seq(zl, y, 1 - c))
    got = taps.at[1 - c]
    copy(got, got, f3_send, f3_recv, seq(zl, y, 1 - c)).wait_recv()

    eye = eye_mask()
    has_halo = s > 0

    for ck, rows in ((1, rows_b), (0, rows_a)):
        k = 1 - ck
        copy(rows.at[1:3, :, 128:256], halo.at[k], h_send.at[k], h_recv.at[k], (g, following)).wait_recv()

        @pl.loop(0, CHAN // CHUNK)
        def _(i, ck=ck, k=k, rows=rows):
            at = pl.ds(pl.multiple_of(i * CHUNK, CHUNK), CHUNK)
            product = rows[1, at, :].astype(F32) * rows[2, at, :].astype(F32)
            before = halo[k, 0, at, :].astype(F32) * halo[k, 1, at, :].astype(F32)
            before = jnp.where(has_halo, before, 0.0)
            window = jnp.concatenate([before, product[:, :128]], axis=1)
            both = jnp.concatenate([window, product], axis=0)
            spectrum = dot3(both, wf_hi[...], wf_lo[...])
            f = jnp.concatenate([taps[d, b, i, ck] for b in range(4) for d in range(2)], axis=0)
            response = dot3(f, wf_hi[:128], wf_lo[:128])
            f_re, f_im = response[:, :128], response[:, 128:]
            parts = []
            for w in range(2):
                x_re = spectrum[w * CHUNK : (w + 1) * CHUNK, :128]
                x_im = spectrum[w * CHUNK : (w + 1) * CHUNK, 128:]
                parts.append(jnp.concatenate([x_re * f_re - x_im * f_im, x_re * f_im + x_im * f_re], axis=1))
            conv = dot3(jnp.concatenate(parts, axis=0), wi_hi[...], wi_lo[...])
            conv = jnp.concatenate([conv[:CHUNK], conv[CHUNK:]], axis=1)
            gated = rows[0, at, :].astype(F32) * conv
            average = jnp.sum(gated, axis=1, keepdims=True) * (1.0 / TOK)
            diff = gated - average
            squares = jnp.sum(diff * diff, axis=1, keepdims=True)
            centred[ck, at, :] = diff
            for h in range(CHUNK // 128):
                own[ck, 0, pl.ds(i * 2 + h, 1), :] = to_row(average[h * 128 : (h + 1) * 128], eye)
                own[ck, 1, pl.ds(i * 2 + h, 1), :] = to_row(squares[h * 128 : (h + 1) * 128], eye)

        level1[ck, y * 2 + c] = own[ck]
        for i in range(1, 8):
            q = lax.rem(y * 2 + c + i, 8)
            go(own.at[ck], level1.at[ck, y * 2 + c], s1_send.at[ck, i], s1_recv.at[ck, y * 2 + c], (g, zl * 8 + q))

    for ck, z in ((1, z_b), (0, z_a)):
        for i in range(1, 8):
            q = lax.rem(y * 2 + c + i, 8)
            copy(own.at[ck], level1.at[ck, q], s1_send.at[ck, i], s1_recv.at[ck, q], (g, zl * 8 + q)).wait_recv()
        mean1 = sum(level1[ck, q, 0] for q in range(8)) * 0.125
        square1 = sum(level1[ck, q, 1] for q in range(8))
        square1 = square1 + TOK * sum((level1[ck, q, 0] - mean1) * (level1[ck, q, 0] - mean1) for q in range(8))
        level2[ck, zl, 0] = mean1
        level2[ck, zl, 1] = square1
        for i, p in enumerate(zl_peers):
            mine = level2.at[ck, zl]
            go(mine, mine, s2_send.at[ck, i], s2_recv.at[ck, zl], seq(p, y, c))
    for ck, z in ((1, z_b), (0, z_a)):
        for p in zl_peers:
            got = level2.at[ck, p]
            copy(got, got, s2_send.at[ck, 0], s2_recv.at[ck, p], seq(p, y, c)).wait_recv()
        mean = sum(level2[ck, p, 0] for p in range(4)) * 0.25
        square = sum(level2[ck, p, 1] for p in range(4))
        square = square + 8 * TOK * sum((level2[ck, p, 0] - mean) * (level2[ck, p, 0] - mean) for p in range(4))
        scale = lax.rsqrt(square * (1.0 / TOKENS) + 1e-05)
        shift = own[ck, 0] - mean
        for j in range(8):
            at = slice(j * 128, (j + 1) * 128)
            shift_c = to_column(shift[j : j + 1], eye)
            scale_c = to_column(scale[j : j + 1], eye)
            z[at, :] = ((centred[ck, at, :] + shift_c) * scale_c).astype(BF)
    for cp in sends:
        cp.wait_send()


def back_kernel(
    z_a, z_b, out, alpha, beta, partial, landed,
    y_send, y_recv, a_send, a_recv, c_send, c_recv, z_send, z_recv, x_send, x_recv, o_send, o_recv, local,
):
    g, s, x, zh, zl, y, c = place()
    me = y * 2 + c
    barrier = pltpu.get_barrier_semaphore()
    x_peers = [lax.rem(x + i, 4) for i in range(1, 4)]
    y_peers = [lax.rem(y + i, 4) for i in range(1, 4)]
    other = (x * 2 + 1 - zh, s)

    @pl.loop(1, 32)
    def _(i):
        pl.semaphore_signal(barrier, inc=1, device_id=(g, lax.rem(s + i, 32)), device_id_type=MESH)

    for p in x_peers:
        pl.semaphore_signal(barrier, inc=1, device_id=(p * 2 + zh, s), device_id_type=MESH)
    pl.semaphore_signal(barrier, inc=1, device_id=other, device_id_type=MESH)
    pl.semaphore_wait(barrier, 35)

    def copy(src, dst, send, recv, device):
        return pltpu.make_async_remote_copy(
            src_ref=src, dst_ref=dst, send_sem=send, recv_sem=recv, device_id=device, device_id_type=MESH
        )

    sends = []

    def go(*args):
        cp = copy(*args)
        cp.start()
        sends.append(cp)

    def columns(q):
        return pl.ds(pl.multiple_of(q * TOK, TOK), TOK)

    def rows(q):
        return pl.ds(pl.multiple_of(q * 128, 128), 128)

    for i in range(1, 8):
        q = lax.rem(me + i, 8)
        go(z_b.at[rows(q)], beta.at[zh, x, :, columns(me)], y_send.at[i], y_recv.at[me], (g, zl * 8 + q))
    keep_b = pltpu.make_async_copy(z_b.at[rows(me)], beta.at[zh, x, :, columns(me)], local.at[0])
    keep_b.start()
    go(z_a, alpha.at[:, columns(me)], c_send.at[0], c_recv.at[y], (g, zl * 8 + y * 2 + 1 - c))
    for i, p in enumerate(y_peers):
        go(z_a, alpha.at[:, columns(me)], a_send.at[i], a_recv.at[y], (g, zl * 8 + p * 2 + c))
    keep_a = pltpu.make_async_copy(z_a, alpha.at[:, columns(me)], local.at[1])
    keep_a.start()
    keep_b.wait()
    for i in range(1, 8):
        q = lax.rem(me + i, 8)
        copy(z_b.at[rows(me)], beta.at[zh, x, :, columns(q)], y_send.at[i], y_recv.at[q], (g, zl * 8 + q)).wait_recv()
    panel = beta.at[zh, x]
    go(panel, panel, z_send, z_recv, other)
    for i, p in enumerate(x_peers):
        go(panel, panel, x_send.at[0, i], x_recv.at[0, x], (p * 2 + zh, s))
    for i, p in enumerate(y_peers):
        got = alpha.at[:, columns(p * 2 + c)]
        copy(z_a, got, a_send.at[i], a_recv.at[p], (g, zl * 8 + p * 2 + c)).wait_recv()
        go(got, got, c_send.at[1 + i], c_recv.at[p], (g, zl * 8 + y * 2 + 1 - c))
    far = beta.at[1 - zh, x]
    copy(far, far, z_send, z_recv, other).wait_recv()
    for i, p in enumerate(x_peers):
        go(far, far, x_send.at[1, i], x_recv.at[1, x], (p * 2 + zh, s))
    keep_a.wait()
    for p in range(4):
        got = alpha.at[:, columns(p * 2 + 1 - c)]
        copy(got, got, c_send.at[0], c_recv.at[p], (g, zl * 8 + y * 2 + 1 - c)).wait_recv()
    for half in range(2):
        zz = zh if half == 0 else 1 - zh
        for p in x_peers:
            got = beta.at[zz, p]
            copy(got, got, x_send.at[half, 0], x_recv.at[half, p], (p * 2 + zh, s)).wait_recv()

        @pl.loop(0, 4)
        def _(i, half=half, zz=zz):
            at = pl.ds(pl.multiple_of(i * 256, 256), 256)
            right = beta[zz].reshape(512, 8 * TOK)
            block = lax.dot_general(alpha[at, :], right, (((1,), (1,)), ((), ())), preferred_element_type=F32)
            partial[half, at, :] = (block * (1.0 / TOKENS)).astype(BF)

        landed[half, s] = partial[half, pl.ds(pl.multiple_of(s * 32, 32), 32), :]

        @pl.loop(1, 32)
        def _(i, half=half):
            t = lax.rem(s + i, 32)
            at = pl.ds(pl.multiple_of(t * 32, 32), 32)
            copy(partial.at[half, at], landed.at[half, s], o_send.at[half, i], o_recv.at[half, s], (g, t)).start()

    for half in range(2):
        zz = zh if half == 0 else 1 - zh

        @pl.loop(1, 32)
        def _(i, half=half):
            t = lax.rem(s + i, 32)
            at = pl.ds(pl.multiple_of(t * 32, 32), 32)
            copy(partial.at[half, at], landed.at[half, t], o_send.at[half, i], o_recv.at[half, t], (g, t)).wait_recv()

        @pl.loop(0, 8)
        def _(q, half=half, zz=zz):
            total = landed[half, q].astype(F32)
            for p in range(1, 4):
                total = total + landed[half, p * 8 + q].astype(F32)
            for p in range(4):
                at = pl.multiple_of((p * 2 + zz) * 1024 + q * 128, 128)
                out[:, pl.ds(at, 128)] = total[:, p * 128 : (p + 1) * 128]

    @pl.loop(1, 32)
    def _(i):
        for half in range(2):
            t = lax.rem(s + i, 32)
            at = pl.ds(pl.multiple_of(t * 32, 32), 32)
            copy(partial.at[half, at], landed.at[half, s], o_send.at[half, i], o_recv.at[half, s], (g, t)).wait_send()

    for cp in sends:
        cp.wait_send()


VMEM = pl.BlockSpec(memory_space=pltpu.VMEM)
DMA = pltpu.SemaphoreType.DMA


def front(rows_a, rows_b, filt_a, filt_b):
    consts = [jnp.asarray(w) for w in dft_constants()]
    return pl.pallas_call(
        front_kernel,
        out_shape=[jax.ShapeDtypeStruct((CHAN, TOK), BF)] * 2,
        in_specs=[VMEM] * 8,
        out_specs=[VMEM] * 2,
        scratch_shapes=[
            pltpu.VMEM((2, 2, CHAN, 128), BF),
            pltpu.VMEM((2, 4, 4, 2, 32, TAPS), F32),
            pltpu.VMEM((2, CHAN, TOK), F32),
            pltpu.VMEM((2, 2, 8, 128), F32),
            pltpu.VMEM((2, 8, 2, 8, 128), F32),
            pltpu.VMEM((2, 4, 2, 8, 128), F32),
            DMA((2,)), DMA((2,)), DMA((3,)), DMA((4,)), DMA((3,)), DMA((4,)), DMA, DMA,
            DMA((2, 8)), DMA((2, 8)), DMA((2, 3)), DMA((2, 4)),
        ],
        compiler_params=pltpu.CompilerParams(
            collective_id=0, has_side_effects=True, vmem_limit_bytes=56 * 2**20
        ),
        name="front",
    )(rows_a, rows_b, filt_a, filt_b, *consts)


def back(z_a, z_b):
    return pl.pallas_call(
        back_kernel,
        out_shape=jax.ShapeDtypeStruct((32, 8 * CHAN), F32),
        in_specs=[VMEM] * 2,
        out_specs=VMEM,
        scratch_shapes=[
            pltpu.VMEM((CHAN, 8 * TOK), BF),
            pltpu.VMEM((2, 4, 128, 8 * TOK), BF),
            pltpu.VMEM((2, CHAN, 512), BF),
            pltpu.VMEM((2, 32, 32, 512), BF),
            DMA((8,)), DMA((8,)), DMA((3,)), DMA((4,)), DMA((4,)), DMA((4,)), DMA, DMA,
            DMA((2, 3)), DMA((2, 4)), DMA((2, 32)), DMA((2, 32)), DMA((2,)),
        ],
        compiler_params=pltpu.CompilerParams(
            collective_id=1, has_side_effects=True, vmem_limit_bytes=56 * 2**20
        ),
        name="back",
    )(z_a, z_b)


def body(rows_alpha, rows_beta, filter_alpha, filter_beta):
    z_a, z_b = front(rows_alpha, rows_beta, filter_alpha, filter_beta)
    return back(z_a, z_b)


def solution(mesh):
    placed = (
        P(None, "grp", "seq"),
        P(None, "grp", "seq"),
        P(("grp", "seq"), None),
        P(("grp", "seq"), None),
    )
    return jax.shard_map(
        body, mesh=mesh, in_specs=placed, out_specs=P(("grp", "seq"), None), check_vma=False
    )
```

time: 514 us -> 146 us (0.28)
  the two profiles are of different devices: /device:TPU:4 before, /device:TPU:41 now
where the time goes in v1:
time: 146 us; the launch traced here: 144 us
  Pallas kernels  141 us (97%)
  local copies, waits for them, and re-layouts  2.26 us (2%)
    pallas_call x1, Pallas kernels, back(): pl.pallas_call(back_kernel, out_shape=jax.ShapeDtypeStruct((32, 8 * CHAN)...  95.7 us
    pallas_call x1, Pallas kernels, front(): pl.pallas_call(front_kernel, out_shape=[jax.ShapeDtypeStruct((CHAN, TOK),...  45.5 us

profile of v1, /device:TPU:41, one launch (start us, length us, event | category | flops | bytes accessed | tf_op | source)
XLA Modules:
  0.0 143.5 jit_solution(8353221960679729377)
XLA Ops:
  0.0 45.5 %front.1 = (bf16[1024,256]{1,0:T(8,128)(2,1)}, bf16[1024,256]{1,0:T(8,128)(2,1)}) custom-call(bf16[3,1024,256]{2,1,0:T(8,128)(2,1)} %rows_a.1, bf16[3,1024,256]{2,1,0:T(8,128)(2,1)} %rows_b.1, f32[32,128]{1,0:T(8,128)} %filt_a.1, f32[32,128]{1,0:T(8,128)} %filt_b.1, bf16[256,256]{1,0:T(8,128)(2,1)} %constant.8.clone.wf_hi, ...), custom_call_target="tpu_custom_call" | custom-call | tf_op jit(solution)/shard_map/front/pallas_call | solution.py:318
  45.5 95.7 %back.1 = f32[32,8192]{1,0:T(8,128)} custom-call(bf16[1024,256]{1,0:T(8,128)(2,1)} %get-tuple-element.7.z_a, bf16[1024,256]{1,0:T(8,128)(2,1)} %get-tuple-element.8.z_b), custom_call_target="tpu_custom_call" | custom-call | tf_op jit(solution)/shard_map/back/pallas_call | solution.py:341
  141.3 2.3 %copy.10 = f32[32,8192]{1,0:T(8,128)} copy(f32[32,8192]{1,0:T(8,128)} %back.1) | data formatting | bytes 2097152

commit v2 on v0

v2 whole, which is shorter than its diff:
```python
import jax
import jax.numpy as jnp
import ml_dtypes
import numpy as np
from jax import lax
from jax.experimental import pallas as pl
from jax.experimental.pallas import tpu as pltpu
from jax.sharding import PartitionSpec as P

MESH = pl.DeviceIdType.MESH
BF = jnp.bfloat16
F32 = jnp.float32
TOKENS = 8192
CHAN = 1024
TOK = 256
TAPS = 128
CHUNK = 256


def split_const(matrix):
    high = matrix.astype(ml_dtypes.bfloat16)
    low = (matrix - high.astype(np.float64)).astype(ml_dtypes.bfloat16)
    return high, low


def dft_constants():
    n = np.arange(256)[:, None]
    k = np.arange(128)[None, :] + 0.5
    angle = 2.0 * np.pi * n * k / 256.0
    forward = np.concatenate([np.cos(angle), -np.sin(angle)], axis=1)
    back = angle[128:].T
    inverse = np.concatenate([np.cos(back), -np.sin(back)], axis=0) / 128.0
    return split_const(forward) + split_const(inverse)


def split(value):
    high = value.astype(BF)
    low = (value - high.astype(F32)).astype(BF)
    return high, low


def dot3(value, w_high, w_low):
    high, low = split(value)
    total = jnp.dot(low, w_high, preferred_element_type=F32)
    total = total + jnp.dot(high, w_low, preferred_element_type=F32)
    return total + jnp.dot(high, w_high, preferred_element_type=F32)


def place():
    g = lax.axis_index("grp")
    s = lax.axis_index("seq")
    return g, s, g // 2, g % 2, s // 8, (s // 2) % 4, s % 2


def eye_mask():
    r = lax.broadcasted_iota(jnp.int32, (128, 128), 0)
    c = lax.broadcasted_iota(jnp.int32, (128, 128), 1)
    return r == c


def to_row(column, eye):
    return jnp.sum(jnp.where(eye, jnp.broadcast_to(column, (128, 128)), 0.0), axis=0, keepdims=True)


def to_column(row, eye):
    return jnp.sum(jnp.where(eye, jnp.broadcast_to(row, (128, 128)), 0.0), axis=1, keepdims=True)


def kernel(
    all_a, all_b, filt_a, filt_b, wf_hi, wf_lo, wi_hi, wi_lo, out,
    kept, edge, halo, taps, centred, z_a, z_b, across, own, level1, level2, shifts, panel, pick, sums, alpha, beta,
    partial, exact, passed, landed,
    h_send, h_recv, f1_send, f1_recv, f2_send, f2_recv, f3_send, f3_recv, s1_send, s1_recv, s2_send, s2_recv,
    y_send, y_recv, w_send, w_recv, a_send, a_recv, c_send, c_recv, z_send, z_recv, x_send, x_recv, p_send, p_recv, r_send, r_recv, o_send, o_recv,
    local, l_sem,
):
    g, s, x, zh, zl, y, c = place()
    me = y * 2 + c
    zl_peers = [lax.rem(zl + i, 4) for i in range(1, 4)]
    y_peers = [lax.rem(y + i, 4) for i in range(1, 4)]
    x_peers = [lax.rem(x + i, 4) for i in range(1, 4)]
    sibling = (g, zl * 8 + y * 2 + 1 - c)
    other = (x * 2 + 1 - zh, s)

    side = zl // 2
    mate = side * 4 + 1 - zl
    outer = (zl + 1) % 4 < 2

    def chunk_at(k):
        far, near = 3 - 3 * side + (k % 2) * (2 * side - 1), mate + (k % 2) * (zl - mate)
        return (1 - k // 2) * far + (k // 2) * near

    def seq(a, b, d):
        return (g, a * 8 + b * 2 + d)

    barrier = pltpu.get_barrier_semaphore()

    def greet(device):
        pl.semaphore_signal(barrier, inc=1, device_id=device, device_id_type=MESH)

    @pl.loop(1, 32)
    def _(i):
        greet((g, lax.rem(s + i, 32)))

    for p in x_peers:
        greet((p * 2 + zh, s))
    greet(other)
    rows_a, rows_b = kept.at[0], kept.at[1]
    loads = []
    for ck, whole in ((1, all_b), (0, all_a)):
        for part in ((1, 3), (0, 1)):
            at = pl.ds(part[0], part[1] - part[0])
            load = pltpu.make_async_copy(whole.at[at], kept.at[ck, at], l_sem.at[ck, part[0]])
            load.start()
            loads.append(load)
    taps[0, c, y, zl] = filt_a[...]
    taps[1, c, y, zl] = filt_b[...]
    for ck in (1, 0):
        loads[2 - 2 * ck].wait()
        edge[ck] = (kept[ck, 1, :, 128:].astype(F32) * kept[ck, 2, :, 128:].astype(F32)).astype(BF)
    pl.semaphore_wait(barrier, 35)

    def copy(src, dst, send, recv, device):
        return pltpu.make_async_remote_copy(
            src_ref=src, dst_ref=dst, send_sem=send, recv_sem=recv, device_id=device, device_id_type=MESH
        )

    sends = []

    def go(*args):
        cp = copy(*args)
        cp.start()
        sends.append(cp)

    def arrive(dst, recv):
        copy(dst, dst, h_send.at[0], recv, sibling).wait_recv()

    def columns(q):
        return pl.ds(pl.multiple_of(q * TOK, TOK), TOK)

    def channels(q):
        return pl.ds(pl.multiple_of(q * 128, 128), 128)

    def chunk(i):
        return pl.ds(pl.multiple_of(i * CHUNK, CHUNK), CHUNK)

    def halo_out(ck):
        go(edge.at[ck], halo.at[ck], h_send.at[ck], h_recv.at[ck], (g, lax.rem(s + 1, 32)))

    def taps_copy(ck, i, p):
        mine = taps.at[ck, c, y]
        return copy(mine, mine, f2_send.at[ck, i], f2_recv.at[ck, y], seq(zl, p, c))

    for ck in (1, 0):
        for i, p in enumerate(zl_peers):
            mine = taps.at[ck, c, y, zl]
            go(mine, mine, f1_send.at[ck, i], f1_recv.at[ck, zl], seq(p, y, c))
        if ck == 1:
            halo_out(1)
    for ck in (1, 0):
        for p in zl_peers:
            arrive(taps.at[ck, c, y, p], f1_recv.at[ck, p])
        first = [taps_copy(ck, i, p) for i, p in enumerate(y_peers)]
        for cp in first:
            cp.start()
        if ck == 1:
            for cp in first:
                cp.wait_send()
            halo_out(0)
        else:
            sends.extend(first)

    lane = lax.broadcasted_iota(jnp.int32, (8 * TOK, 128), 1)
    slot = lax.broadcasted_iota(jnp.int32, (8 * TOK, 128), 0) // TOK
    pick[...] = jnp.where((lane < 24) & (lane % 8 == slot), 1.0, 0.0).astype(BF)

    eye = eye_mask()
    has_halo = s > 0

    def convolve(ck, rows, i):
        at = chunk(i)
        product = rows[1, at, :].astype(F32) * rows[2, at, :].astype(F32)
        before = jnp.where(has_halo, halo[ck, at, :].astype(F32), 0.0)
        window = jnp.concatenate([before, product[:, :128]], axis=1)
        spectrum = dot3(jnp.concatenate([window, product], axis=0), wf_hi[...], wf_lo[...])
        f = jnp.concatenate([taps[ck, d, b, i] for b in range(4) for d in range(2)], axis=0)
        response = dot3(f, wf_hi[:128], wf_lo[:128])
        f_re, f_im = response[:, :128], response[:, 128:]
        parts = []
        for w in range(2):
            x_re = spectrum[w * CHUNK : (w + 1) * CHUNK, :128]
            x_im = spectrum[w * CHUNK : (w + 1) * CHUNK, 128:]
            parts.append(jnp.concatenate([x_re * f_re - x_im * f_im, x_re * f_im + x_im * f_re], axis=1))
        conv = dot3(jnp.concatenate(parts, axis=0), wi_hi[...], wi_lo[...])
        conv = jnp.concatenate([conv[:CHUNK], conv[CHUNK:]], axis=1)
        gated = rows[0, at, :].astype(F32) * conv
        average = jnp.sum(gated, axis=1, keepdims=True) * (1.0 / TOK)
        diff = gated - average
        squares = jnp.sum(diff * diff, axis=1, keepdims=True)
        for h in range(CHUNK // 128):
            own[ck, 0, pl.ds(i * 2 + h, 1), :] = to_row(average[h * 128 : (h + 1) * 128], eye)
            own[ck, 1, pl.ds(i * 2 + h, 1), :] = to_row(squares[h * 128 : (h + 1) * 128], eye)
        return diff

    def to_sibling(ck):
        return copy(taps.at[ck, c], taps.at[ck, c], f3_send.at[ck], f3_recv.at[ck], sibling)

    def filters_half(ck):
        for p in y_peers:
            arrive(taps.at[ck, c, p], f2_recv.at[ck, p])
        to_sibling(ck).start()

    def filters_rest(ck):
        arrive(taps.at[ck, 1 - c], f3_recv.at[ck])
        arrive(halo.at[ck], h_recv.at[ck])

    def over_z(k):
        at = pl.ds(lax.rem(y + 1 + k, 4) * 2, 2)
        return copy(z_b.at[at], across.at[at], z_send.at[k], z_recv.at[k], other)

    def share(far, q):
        src, zz = (across, 1 - zh) if far else (z_b, zh)
        dst = beta.at[zz, columns(me), channels(x)]
        send, recv = (w_send, w_recv) if far else (y_send, y_recv)
        return copy(src.at[q], dst, send.at[q], recv.at[me], (g, zl * 8 + q))

    def relay_z(k):
        i = lax.rem(y + 1 + k, 4)
        arrive(across.at[pl.ds(i * 2, 2)], z_recv.at[k])
        for h in range(2):
            q = i * 2 + h

            @pl.when(q != me)
            def _(q=q):
                share(1, q).start()

    filters_half(1)
    filters_rest(1)
    loads[1].wait()

    @pl.loop(0, 4)
    def _(k):
        @pl.when(k == 2)
        def _():
            filters_half(0)

        i = lax.rem(y + 1 + k, 4)
        turned = convolve(1, rows_b, i).T.astype(BF)
        for h in range(2):
            z_b[i * 2 + h] = turned[:, h * 128 : (h + 1) * 128]
        over_z(k).start()
        for h in range(2):
            q = i * 2 + h

            @pl.when(q != me)
            def _(q=q):
                share(0, q).start()

    keep_b = pltpu.make_async_copy(z_b.at[me], beta.at[zh, columns(me), channels(x)], local.at[0])
    keep_b.start()

    filters_rest(0)
    loads[3].wait()

    @pl.loop(0, 4)
    def _(i):
        centred[chunk(i), :] = convolve(0, rows_a, i)

    level1[me] = own[...]
    for i in range(1, 8):
        q = lax.rem(me + i, 8)
        go(own, level1.at[me], s1_send.at[i], s1_recv.at[me], (g, zl * 8 + q))

    keep_b.wait()
    for i in range(1, 8):
        q = lax.rem(me + i, 8)
        arrive(beta.at[zh, columns(q), channels(x)], y_recv.at[q])
    up, down = (lax.rem(x + 1, 4) * 2 + zh, s), (lax.rem(x + 3, 4) * 2 + zh, s)

    def piece(far, step, part):
        zz = 1 - zh if far else zh
        return beta.at[zz, pl.ds(part * 1024, 1024), channels(lax.rem(x + step, 4))]

    def spread_x(far, part):
        src = piece(far, 0, part)
        for i, device in enumerate((up, down)):
            go(src, src, x_send.at[far, i, part], x_recv.at[far, 2 - 2 * i, part], device)

    def pass_on(far, part):
        src = piece(far, 3 - 2 * part, part)
        return copy(src, src, x_send.at[far, 2, part], x_recv.at[far, 1, part], down if part else up)

    def relay_x(far):
        for part in range(2):
            arrive(piece(far, 3 - 2 * part, part), x_recv.at[far, 2 - 2 * part, part])
            pass_on(far, part).start()

    def rest_x(far):
        for step, part in ((1, 0), (3, 1), (2, 0), (2, 1)):
            arrive(piece(far, step, part), x_recv.at[far, step - 1, part])

    for part in range(2):
        spread_x(0, part)

    for i in range(1, 8):
        q = lax.rem(me + i, 8)
        arrive(level1.at[q], s1_recv.at[q])
    for ck in range(2):
        mean1 = sum(level1[q, ck, 0] for q in range(8)) * 0.125
        square1 = sum(level1[q, ck, 1] for q in range(8))
        square1 = square1 + TOK * sum(
            (level1[q, ck, 0] - mean1) * (level1[q, ck, 0] - mean1) for q in range(8)
        )
        level2[zl, ck, 0] = mean1
        level2[zl, ck, 1] = square1
    for i, p in enumerate(zl_peers):
        go(level2.at[zl], level2.at[zl], s2_send.at[i], s2_recv.at[zl], seq(p, y, c))
    for p in zl_peers:
        arrive(level2.at[p], s2_recv.at[p])
    for ck in range(2):
        mean = sum(level2[p, ck, 0] for p in range(4)) * 0.25
        square = sum(level2[p, ck, 1] for p in range(4))
        square = square + 8 * TOK * sum(
            (level2[p, ck, 0] - mean) * (level2[p, ck, 0] - mean) for p in range(4)
        )
        scale = lax.rsqrt(square * (1.0 / TOKENS) + 1e-05)
        shifts[ck, 0] = own[0, 0] - mean if ck == 0 else mean
        shifts[ck, 1] = scale

    def alpha_out(k):
        at = chunk(chunk_at(k))
        src, dst = z_a.at[at], alpha.at[at, columns(me)]
        for j, p in enumerate(y_peers):
            go(src, dst, a_send.at[k, j], a_recv.at[k, y], seq(zl, p, c))
        go(src, dst, c_send.at[k, y], c_recv.at[k, y], sibling)

    for k in range(4):
        for h in range(2):
            block = chunk_at(k) * 2 + h
            shift_c = to_column(shifts[0, 0, pl.ds(block, 1), :], eye)
            scale_c = to_column(shifts[0, 1, pl.ds(block, 1), :], eye)
            z_a[channels(block), :] = ((centred[channels(block), :] + shift_c) * scale_c).astype(BF)
        if k < 2:
            alpha_out(k)
    keep_a = pltpu.make_async_copy(z_a, alpha.at[:, columns(me)], local.at[1])
    keep_a.start()

    mean_b = shifts[1, 0, pl.ds(me, 1), :]
    for q in range(8):
        panel[zh, x, q : q + 1, :] = level1[q, 1, 0, pl.ds(me, 1), :] - mean_b
    panel[zh, x, 8:9, :] = shifts[1, 1, pl.ds(me, 1), :]
    panel[zh, x, 9:16, :] = jnp.zeros((7, 128), F32)
    mine = panel.at[zh, x]
    go(mine, mine, p_send.at[6], p_recv.at[1, x], other)
    for i, p in enumerate(x_peers):
        go(mine, mine, p_send.at[i], p_recv.at[0, x], (p * 2 + zh, s))

    def alpha_slot(k, p, d):
        return alpha.at[chunk(chunk_at(k)), columns(p * 2 + d)]

    def alpha_copy(k, p):
        got = alpha_slot(k, p, c)
        return copy(got, got, c_send.at[k, p], c_recv.at[k, p], sibling)

    def relay_alpha(k):
        for p in y_peers:
            arrive(alpha_slot(k, p, c), a_recv.at[k, p])
            alpha_copy(k, p).start()

    relay_x(0)
    for k in range(4):
        relay_z(k)
    keep_f = pltpu.make_async_copy(across.at[me], beta.at[1 - zh, columns(me), channels(x)], local.at[0])
    keep_f.start()
    relay_alpha(0)
    keep_f.wait()
    for i in range(1, 8):
        q = lax.rem(me + i, 8)
        arrive(beta.at[1 - zh, columns(q), channels(x)], w_recv.at[q])
    for part in range(2):
        spread_x(1, part)
    alpha_out(2)
    alpha_out(3)
    relay_alpha(1)
    mine = panel.at[1 - zh, x]
    arrive(mine, p_recv.at[1, x])
    for i, p in enumerate(x_peers):
        go(mine, mine, p_send.at[3 + i], p_recv.at[2, x], (p * 2 + zh, s))
    keep_a.wait()

    lane = lax.broadcasted_iota(jnp.int32, (CHUNK, 128), 1)
    low_lanes = (lane >= 8) & (lane < 16)

    def hand(half, k):
        return copy(
            partial.at[half, chunk(chunk_at(k))], passed.at[half, k], r_send.at[half, k], r_recv.at[half, k],
            (g, mate * 8 + me),
        )

    def deliver(half, k, q):
        i = chunk_at(k)
        src = partial.at[half, pl.ds(pl.multiple_of((i * 8 + q) * 32, 32), 32)]
        kind = 2 * (1 - k // 2) + (k // 2) * (1 - k % 2)
        return copy(src, landed.at[half, kind, me], o_send.at[half, k, q], o_recv.at[half, kind, me], (g, i * 8 + q))

    def deliver_all(half, k):
        @pl.loop(0, 8)
        def _(j):
            deliver(half, k, lax.rem(me + j, 8)).start()

    def join(half, k):
        @pl.when(jnp.logical_not(outer))
        def _():
            arrive(passed.at[half, k], r_recv.at[half, k])
            at = chunk(chunk_at(k))
            partial[half, at, :] = (exact[k] + passed[half, k].astype(F32)).astype(BF)
            deliver_all(half, k)

    for half in range(2):
        zz = zh if half == 0 else 1 - zh
        rest_x(half)
        for p in x_peers:
            arrive(panel.at[zz, p], p_recv.at[2 * half, p])
        delta = jnp.concatenate([panel[zz, p, 0:8, :] for p in range(4)], axis=1)
        weight = jnp.concatenate([panel[zz, p, 8:9, :] for p in range(4)], axis=1) * (1.0 / TOKENS)
        delta_hi = delta.astype(BF).astype(F32)
        spread = jnp.concatenate(
            [delta_hi, delta_hi, delta - delta_hi, jnp.zeros((104, 512), F32)], axis=0
        ).astype(BF)

        @pl.loop(0, 4)
        def _(k, half=half, zz=zz, spread=spread, weight=weight):
            at = chunk(chunk_at(k))

            @pl.when(k >= 2)
            def _():
                join(half, k - 2)

            if half == 0:
                for p in range(4):
                    arrive(alpha_slot(k, p, 1 - c), c_recv.at[k, p])
                total = jnp.dot(alpha[at, :], pick[...], preferred_element_type=F32)
                total_hi = total.astype(BF).astype(F32)
                sums[at, :] = jnp.where(low_lanes, total - total_hi, total_hi).astype(BF)
            block = jnp.dot(alpha[at, :], beta[zz], preferred_element_type=F32)
            block = block + jnp.dot(sums[at, :], spread, preferred_element_type=F32)
            block = block * weight
            partial[half, at, :] = block.astype(BF)

            @pl.when(k < 2)
            def _():
                exact[k] = block

                @pl.when(outer)
                def _():
                    hand(half, k).start()

                if half == 0:
                    relay_alpha(k + 2)

                    @pl.when(k == 1)
                    def _():
                        relay_x(1)

            @pl.when(k == 2)
            def _():
                deliver_all(half, 2)

        @pl.loop(1, 8)
        def _(j, half=half):
            deliver(half, 3, lax.rem(me + j, 8)).start()

        landed[half, 0, me] = partial[half, pl.ds(pl.multiple_of(s * 32, 32), 32), :]

    for half in range(2):
        zz = zh if half == 0 else 1 - zh

        @pl.loop(1, 8)
        def _(j, half=half):
            q = lax.rem(me + j, 8)
            arrive(landed.at[half, 0, q], o_recv.at[half, 0, q])

        @pl.loop(0, 8)
        def _(q, half=half, zz=zz):
            for kind in (1, 2):
                arrive(landed.at[half, kind, q], o_recv.at[half, kind, q])
            total = landed[half, 0, q].astype(F32) + landed[half, 1, q].astype(F32)
            total = total + landed[half, 2, q].astype(F32)
            for p in range(4):
                at = pl.multiple_of((p * 2 + zz) * 1024 + q * 128, 128)
                out[:, pl.ds(at, 128)] = total[:, p * 128 : (p + 1) * 128]

    for half in range(2):
        for k in range(4):

            @pl.loop(1 if k == 3 else 0, 8)
            def _(j, half=half, k=k):
                @pl.when(jnp.logical_not(outer) | (k >= 2))
                def _():
                    deliver(half, k, lax.rem(me + j, 8)).wait_send()

        @pl.when(outer)
        def _(half=half):
            for k in range(2):
                hand(half, k).wait_send()

    @pl.loop(1, 8)
    def _(i):
        q = lax.rem(me + i, 8)
        share(0, q).wait_send()
        share(1, q).wait_send()

    for k in range(4):
        over_z(k).wait_send()
    for far in range(2):
        for part in range(2):
            pass_on(far, part).wait_send()
    for ck in range(2):
        to_sibling(ck).wait_send()
    for k in range(4):
        for p in y_peers:
            alpha_copy(k, p).wait_send()
    for cp in sends:
        cp.wait_send()


VMEM = pl.BlockSpec(memory_space=pltpu.VMEM)
DMA = pltpu.SemaphoreType.DMA


def body(rows_alpha, rows_beta, filter_alpha, filter_beta):
    consts = [jnp.asarray(w) for w in dft_constants()]
    return pl.pallas_call(
        kernel,
        out_shape=jax.ShapeDtypeStruct((32, 8 * CHAN), F32),
        in_specs=[pl.BlockSpec(memory_space=pl.ANY)] * 2 + [VMEM] * 6,
        out_specs=VMEM,
        scratch_shapes=[
            pltpu.VMEM((2, 3, CHAN, TOK), BF),
            pltpu.VMEM((2, CHAN, 128), BF),
            pltpu.VMEM((2, CHAN, 128), BF),
            pltpu.VMEM((2, 2, 4, 4, 32, TAPS), F32),
            pltpu.VMEM((CHAN, TOK), F32),
            pltpu.VMEM((CHAN, TOK), BF),
            pltpu.VMEM((8, TOK, 128), BF),
            pltpu.VMEM((8, TOK, 128), BF),
            pltpu.VMEM((2, 2, 8, 128), F32),
            pltpu.VMEM((8, 2, 2, 8, 128), F32),
            pltpu.VMEM((4, 2, 2, 8, 128), F32),
            pltpu.VMEM((2, 2, 8, 128), F32),
            pltpu.VMEM((2, 4, 16, 128), F32),
            pltpu.VMEM((8 * TOK, 128), BF),
            pltpu.VMEM((CHAN, 128), BF),
            pltpu.VMEM((CHAN, 8 * TOK), BF),
            pltpu.VMEM((2, 8 * TOK, 512), BF),
            pltpu.VMEM((2, CHAN, 512), BF),
            pltpu.VMEM((2, CHUNK, 512), F32),
            pltpu.VMEM((2, 2, CHUNK, 512), BF),
            pltpu.VMEM((2, 3, 8, 32, 512), BF),
            DMA((2,)), DMA((2,)), DMA((2, 3)), DMA((2, 4)), DMA((2, 3)), DMA((2, 4)), DMA((2,)), DMA((2,)),
            DMA((8,)), DMA((8,)), DMA((3,)), DMA((4,)),
            DMA((8,)), DMA((8,)), DMA((8,)), DMA((8,)), DMA((4, 3)), DMA((4, 4)), DMA((4, 4)), DMA((4, 4)),
            DMA((4,)), DMA((4,)), DMA((2, 3, 2)), DMA((2, 3, 2)), DMA((7,)), DMA((3, 4)), DMA((2, 2)), DMA((2, 2)),
            DMA((2, 4, 8)), DMA((2, 3, 8)), DMA((2,)), DMA((2, 2)),
        ],
        compiler_params=pltpu.CompilerParams(
            collective_id=0, has_side_effects=True, vmem_limit_bytes=56 * 2**20
        ),
        name="correlate",
    )(rows_alpha, rows_beta, filter_alpha, filter_beta, *consts)


def solution(mesh):
    placed = (
        P(None, "grp", "seq"),
        P(None, "grp", "seq"),
        P(("grp", "seq"), None),
        P(("grp", "seq"), None),
    )
    return jax.shard_map(
        body, mesh=mesh, in_specs=placed, out_specs=P(("grp", "seq"), None), check_vma=False
    )
```

time: 514 us -> 128 us (0.25)
  the two profiles are of different devices: /device:TPU:4 before, /device:TPU:161 now
where the time goes in v2:
time: 128 us; the launch traced here: 127 us
  Pallas kernels  125 us (98%)
  local copies, waits for them, and re-layouts  2.26 us (2%)
    pallas_call x1, Pallas kernels, body(): pl.pallas_call(kernel, out_shape=jax.ShapeDtypeStruct((32, 8 * CHAN), F32...  125 us

profile of v2, /device:TPU:161, one launch (start us, length us, event | category | flops | bytes accessed | tf_op | source)
XLA Modules:
  0.0 127.5 jit_solution(16269287213757104726)
XLA Ops:
  0.0 125.2 %correlate.1 = f32[32,8192]{1,0:T(8,128)} custom-call(bf16[3,1024,256]{2,1,0:T(8,128)(2,1)} %all_a.1, bf16[3,1024,256]{2,1,0:T(8,128)(2,1)} %all_b.1, f32[32,128]{1,0:T(8,128)} %filt_a.1, f32[32,128]{1,0:T(8,128)} %filt_b.1, bf16[256,256]{1,0:T(8,128)(2,1)} %constant.8.clone.wf_hi, bf16[256,256]{1,0:T(8,128)(2,1)} %constant.9.clone.wf_lo, ...), custom_call_target="tpu_custom_call" | custom-call | tf_op jit(solution)/shard_map/correlate/pallas_call | solution.py:533
  125.2 2.3 %copy.10 = f32[32,8192]{1,0:T(8,128)} copy(f32[32,8192]{1,0:T(8,128)} %correlate.1) | data formatting | bytes 2097152

commit v3 on v2

--- a/solution.py
+++ b/solution.py
@@ -107,7 +107,7 @@
     greet(other)
     rows_a, rows_b = kept.at[0], kept.at[1]
     loads = []
-    for ck, whole in ((1, all_b), (0, all_a)):
+    for ck, whole in ((0, all_a), (1, all_b)):
         for part in ((1, 3), (0, 1)):
             at = pl.ds(part[0], part[1] - part[0])
             load = pltpu.make_async_copy(whole.at[at], kept.at[ck, at], l_sem.at[ck, part[0]])
@@ -115,8 +115,8 @@
             loads.append(load)
     taps[0, c, y, zl] = filt_a[...]
     taps[1, c, y, zl] = filt_b[...]
-    for ck in (1, 0):
-        loads[2 - 2 * ck].wait()
+    for ck in range(2):
+        loads[2 * ck].wait()
         edge[ck] = (kept[ck, 1, :, 128:].astype(F32) * kept[ck, 2, :, 128:].astype(F32)).astype(BF)
     pl.semaphore_wait(barrier, 35)
 
@@ -151,22 +151,21 @@
         mine = taps.at[ck, c, y]
         return copy(mine, mine, f2_send.at[ck, i], f2_recv.at[ck, y], seq(zl, p, c))
 
-    for ck in (1, 0):
+    for ck in range(2):
         for i, p in enumerate(zl_peers):
             mine = taps.at[ck, c, y, zl]
             go(mine, mine, f1_send.at[ck, i], f1_recv.at[ck, zl], seq(p, y, c))
-        if ck == 1:
-            halo_out(1)
-    for ck in (1, 0):
+    for ck in range(2):
+        halo_out(ck)
+    for ck in range(2):
         for p in zl_peers:
             arrive(taps.at[ck, c, y, p], f1_recv.at[ck, p])
         first = [taps_copy(ck, i, p) for i, p in enumerate(y_peers)]
         for cp in first:
             cp.start()
-        if ck == 1:
+        if ck == 0:
             for cp in first:
                 cp.wait_send()
-            halo_out(0)
         else:
             sends.extend(first)
 
@@ -214,118 +213,121 @@
         arrive(taps.at[ck, 1 - c], f3_recv.at[ck])
         arrive(halo.at[ck], h_recv.at[ck])
 
-    def over_z(k):
+    def over_z(part, k):
         at = pl.ds(lax.rem(y + 1 + k, 4) * 2, 2)
-        return copy(z_b.at[at], across.at[at], z_send.at[k], z_recv.at[k], other)
-
-    def share(far, q):
-        src, zz = (across, 1 - zh) if far else (z_b, zh)
-        dst = beta.at[zz, columns(me), channels(x)]
-        send, recv = (w_send, w_recv) if far else (y_send, y_recv)
-        return copy(src.at[q], dst, send.at[q], recv.at[me], (g, zl * 8 + q))
-
-    def relay_z(k):
-        i = lax.rem(y + 1 + k, 4)
-        arrive(across.at[pl.ds(i * 2, 2)], z_recv.at[k])
-        for h in range(2):
-            q = i * 2 + h
-
-            @pl.when(q != me)
-            def _(q=q):
-                share(1, q).start()
-
+        return copy(z_b.at[part, at], across.at[part, at], z_send.at[part, k], z_recv.at[part, k], other)
+
+    def share_near(q):
+        dst = beta.at[zh, me, :, :, channels(x)]
+        return copy(z_b.at[:, q], dst, y_send.at[q], y_recv.at[me], (g, zl * 8 + q))
+
+    def share_far(part, q):
+        dst = beta.at[1 - zh, me, part, :, channels(x)]
+        return copy(across.at[part, q], dst, w_send.at[part, q], w_recv.at[part, me], (g, zl * 8 + q))
+
+    def relay_z(part):
+        for k in range(4):
+            i = lax.rem(y + 1 + k, 4)
+            arrive(across.at[part, pl.ds(i * 2, 2)], z_recv.at[part, k])
+            for h in range(2):
+                q = i * 2 + h
+
+                @pl.when(q != me)
+                def _(q=q):
+                    share_far(part, q).start()
+
+        keep = pltpu.make_async_copy(across.at[part, me], beta.at[1 - zh, me, part, :, channels(x)], local.at[0])
+        keep.start()
+        keep.wait()
+
+    up, down = (lax.rem(x + 1, 4) * 2 + zh, s), (lax.rem(x + 3, 4) * 2 + zh, s)
+
+    def piece(far, step, part, at=slice(None)):
+        zz = 1 - zh if far else zh
+        return beta.at[zz, at, part, :, channels(lax.rem(x + step, 4))]
+
+    def spread_x(far, part):
+        src = piece(far, 0, part)
+        for i, device in enumerate((up, down)):
+            go(src, src, x_send.at[far, i, part, 0], x_recv.at[far, 2 - 2 * i, part, 0], device)
+
+    def pass_on(far, part, i):
+        src = piece(far, 3 - 2 * i, part, pl.ds(4 * i, 4))
+        return copy(src, src, x_send.at[far, i, part, 1], x_recv.at[far, 1, part, i], down if i else up)
+
+    def relay_x(far, part):
+        for i in range(2):
+            arrive(piece(far, 3 - 2 * i, part), x_recv.at[far, 2 - 2 * i, part, 0])
+            pass_on(far, part, i).start()
+
+    def rest_x(far):
+        for part in range(2):
+            for i in range(2):
+                arrive(piece(far, 2, part, pl.ds(4 * i, 4)), x_recv.at[far, 1, part, i])
+
+    def level_z(ck):
+        level1[zl, ck] = own[ck]
+        for i, p in enumerate(zl_peers):
+            go(own.at[ck], level1.at[zl, ck], s1_send.at[ck, i], s1_recv.at[ck, zl], seq(p, y, c))
+
+    def merge(parts, count):
+        mean = sum(m for m, _ in parts) * (1.0 / len(parts))
+        square = sum(v for _, v in parts)
+        return mean, square + count * sum((m - mean) * (m - mean) for m, _ in parts)
+
+    def level_y(ck):
+        for p in zl_peers:
+            arrive(level1.at[p, ck], s1_recv.at[ck, p])
+        mean, square = merge([(level1[p, ck, 0], level1[p, ck, 1]) for p in range(4)], TOK)
+        level2[me, ck, 0] = mean
+        level2[me, ck, 1] = square
+        level2[me, ck, 2] = own[ck, 0]
+        for i in range(1, 8):
+            q = lax.rem(me + i, 8)
+            mine = level2.at[me, ck]
+            go(mine, mine, s2_send.at[ck, i], s2_recv.at[ck, me], (g, zl * 8 + q))
+
+    def statistics(ck):
+        for i in range(1, 8):
+            q = lax.rem(me + i, 8)
+            arrive(level2.at[q, ck], s2_recv.at[ck, q])
+        mean, square = merge([(level2[q, ck, 0], level2[q, ck, 1]) for q in range(8)], 4 * TOK)
+        shifts[ck, 0] = own[ck, 0] - mean if ck == 0 else mean
+        shifts[ck, 1] = lax.rsqrt(square * (1.0 / TOKENS) + 1e-05)
+
+    filters_half(0)
+    filters_rest(0)
+    loads[1].wait()
+
+    @pl.loop(0, 4)
+    def _(i):
+        centred[chunk(i), :] = convolve(0, rows_a, i)
+
+    level_z(0)
     filters_half(1)
+    level_y(0)
+
     filters_rest(1)
-    loads[1].wait()
+    loads[3].wait()
 
     @pl.loop(0, 4)
     def _(k):
-        @pl.when(k == 2)
-        def _():
-            filters_half(0)
-
         i = lax.rem(y + 1 + k, 4)
         turned = convolve(1, rows_b, i).T.astype(BF)
         for h in range(2):
-            z_b[i * 2 + h] = turned[:, h * 128 : (h + 1) * 128]
-        over_z(k).start()
+            for part in range(2):
+                z_b[part, i * 2 + h] = turned[part * 128 : (part + 1) * 128, h * 128 : (h + 1) * 128]
         for h in range(2):
             q = i * 2 + h
 
             @pl.when(q != me)
             def _(q=q):
-                share(0, q).start()
-
-    keep_b = pltpu.make_async_copy(z_b.at[me], beta.at[zh, columns(me), channels(x)], local.at[0])
+                share_near(q).start()
+
+    keep_b = pltpu.make_async_copy(z_b.at[:, me], beta.at[zh, me, :, :, channels(x)], local.at[0])
     keep_b.start()
-
-    filters_rest(0)
-    loads[3].wait()
-
-    @pl.loop(0, 4)
-    def _(i):
-        centred[chunk(i), :] = convolve(0, rows_a, i)
-
-    level1[me] = own[...]
-    for i in range(1, 8):
-        q = lax.rem(me + i, 8)
-        go(own, level1.at[me], s1_send.at[i], s1_recv.at[me], (g, zl * 8 + q))
-
-    keep_b.wait()
-    for i in range(1, 8):
-        q = lax.rem(me + i, 8)
-        arrive(beta.at[zh, columns(q), channels(x)], y_recv.at[q])
-    up, down = (lax.rem(x + 1, 4) * 2 + zh, s), (lax.rem(x + 3, 4) * 2 + zh, s)
-
-    def piece(far, step, part):
-        zz = 1 - zh if far else zh
-        return beta.at[zz, pl.ds(part * 1024, 1024), channels(lax.rem(x + step, 4))]
-
-    def spread_x(far, part):
-        src = piece(far, 0, part)
-        for i, device in enumerate((up, down)):
-            go(src, src, x_send.at[far, i, part], x_recv.at[far, 2 - 2 * i, part], device)
-
-    def pass_on(far, part):
-        src = piece(far, 3 - 2 * part, part)
-        return copy(src, src, x_send.at[far, 2, part], x_recv.at[far, 1, part], down if part else up)
-
-    def relay_x(far):
-        for part in range(2):
-            arrive(piece(far, 3 - 2 * part, part), x_recv.at[far, 2 - 2 * part, part])
-            pass_on(far, part).start()
-
-    def rest_x(far):
-        for step, part in ((1, 0), (3, 1), (2, 0), (2, 1)):
-            arrive(piece(far, step, part), x_recv.at[far, step - 1, part])
-
-    for part in range(2):
-        spread_x(0, part)
-
-    for i in range(1, 8):
-        q = lax.rem(me + i, 8)
-        arrive(level1.at[q], s1_recv.at[q])
-    for ck in range(2):
-        mean1 = sum(level1[q, ck, 0] for q in range(8)) * 0.125
-        square1 = sum(level1[q, ck, 1] for q in range(8))
-        square1 = square1 + TOK * sum(
-            (level1[q, ck, 0] - mean1) * (level1[q, ck, 0] - mean1) for q in range(8)
-        )
-        level2[zl, ck, 0] = mean1
-        level2[zl, ck, 1] = square1
-    for i, p in enumerate(zl_peers):
-        go(level2.at[zl], level2.at[zl], s2_send.at[i], s2_recv.at[zl], seq(p, y, c))
-    for p in zl_peers:
-        arrive(level2.at[p], s2_recv.at[p])
-    for ck in range(2):
-        mean = sum(level2[p, ck, 0] for p in range(4)) * 0.25
-        square = sum(level2[p, ck, 1] for p in range(4))
-        square = square + 8 * TOK * sum(
-            (level2[p, ck, 0] - mean) * (level2[p, ck, 0] - mean) for p in range(4)
-        )
-        scale = lax.rsqrt(square * (1.0 / TOKENS) + 1e-05)
-        shifts[ck, 0] = own[0, 0] - mean if ck == 0 else mean
-        shifts[ck, 1] = scale
+    level_z(1)
+    statistics(0)
 
     def alpha_out(k):
         at = chunk(chunk_at(k))
@@ -340,14 +342,29 @@
             shift_c = to_column(shifts[0, 0, pl.ds(block, 1), :], eye)
             scale_c = to_column(shifts[0, 1, pl.ds(block, 1), :], eye)
             z_a[channels(block), :] = ((centred[channels(block), :] + shift_c) * scale_c).astype(BF)
-        if k < 2:
-            alpha_out(k)
+    level_y(1)
+    for k in range(4):
+        over_z(0, k).start()
+    alpha_out(0)
+    alpha_out(1)
     keep_a = pltpu.make_async_copy(z_a, alpha.at[:, columns(me)], local.at[1])
     keep_a.start()
 
+    keep_b.wait()
+    for i in range(1, 8):
+        q = lax.rem(me + i, 8)
+        arrive(beta.at[zh, q, :, :, channels(x)], y_recv.at[q])
+    for part in range(2):
+        spread_x(0, part)
+    alpha_out(2)
+    relay_x(0, 0)
+    for k in range(4):
+        over_z(1, k).start()
+    statistics(1)
+
     mean_b = shifts[1, 0, pl.ds(me, 1), :]
     for q in range(8):
-        panel[zh, x, q : q + 1, :] = level1[q, 1, 0, pl.ds(me, 1), :] - mean_b
+        panel[zh, x, q : q + 1, :] = level2[q, 1, 2, pl.ds(me, 1), :] - mean_b
     panel[zh, x, 8:9, :] = shifts[1, 1, pl.ds(me, 1), :]
     panel[zh, x, 9:16, :] = jnp.zeros((7, 128), F32)
     mine = panel.at[zh, x]
@@ -367,34 +384,30 @@
             arrive(alpha_slot(k, p, c), a_recv.at[k, p])
             alpha_copy(k, p).start()
 
-    relay_x(0)
-    for k in range(4):
-        relay_z(k)
-    keep_f = pltpu.make_async_copy(across.at[me], beta.at[1 - zh, columns(me), channels(x)], local.at[0])
-    keep_f.start()
+    def far_in(part):
+        for i in range(1, 8):
+            q = lax.rem(me + i, 8)
+            arrive(beta.at[1 - zh, q, part, :, channels(x)], w_recv.at[part, q])
+        spread_x(1, part)
+
+    relay_z(0)
+    alpha_out(3)
+    relay_x(0, 1)
+    far_in(0)
     relay_alpha(0)
-    keep_f.wait()
-    for i in range(1, 8):
-        q = lax.rem(me + i, 8)
-        arrive(beta.at[1 - zh, columns(q), channels(x)], w_recv.at[q])
-    for part in range(2):
-        spread_x(1, part)
-    alpha_out(2)
-    alpha_out(3)
     relay_alpha(1)
-    mine = panel.at[1 - zh, x]
-    arrive(mine, p_recv.at[1, x])
-    for i, p in enumerate(x_peers):
-        go(mine, mine, p_send.at[3 + i], p_recv.at[2, x], (p * 2 + zh, s))
+    relay_z(1)
+    relay_alpha(2)
     keep_a.wait()
 
     lane = lax.broadcasted_iota(jnp.int32, (CHUNK, 128), 1)
     low_lanes = (lane >= 8) & (lane < 16)
 
-    def hand(half, k):
+    def hand(half, k, part):
+        rows = pl.ds(pl.multiple_of(chunk_at(k) * CHUNK + part * 128, 128), 128)
         return copy(
-            partial.at[half, chunk(chunk_at(k))], passed.at[half, k], r_send.at[half, k], r_recv.at[half, k],
-            (g, mate * 8 + me),
+            partial.at[half, rows], passed.at[half, k, pl.ds(part * 128, 128)],
+            r_send.at[half, k, part], r_recv.at[half, k, part], (g, mate * 8 + me),
         )
 
     def deliver(half, k, q):
@@ -411,12 +424,17 @@
     def join(half, k):
         @pl.when(jnp.logical_not(outer))
         def _():
-            arrive(passed.at[half, k], r_recv.at[half, k])
-            at = chunk(chunk_at(k))
-            partial[half, at, :] = (exact[k] + passed[half, k].astype(F32)).astype(BF)
-            deliver_all(half, k)
-
-    for half in range(2):
+            for part in range(2):
+                rows = pl.ds(part * 128, 128)
+                arrive(passed.at[half, k, rows], r_recv.at[half, k, part])
+                at = pl.ds(pl.multiple_of(chunk_at(k) * CHUNK + part * 128, 128), 128)
+                partial[half, at, :] = (exact[k, rows, :] + passed[half, k, rows, :].astype(F32)).astype(BF)
+
+                @pl.loop(0, 4)
+                def _(j, part=part):
+                    deliver(half, k, part * 4 + lax.rem(me + j, 4)).start()
+
+    def columns_in(half):
         zz = zh if half == 0 else 1 - zh
         rest_x(half)
         for p in x_peers:
@@ -427,50 +445,64 @@
         spread = jnp.concatenate(
             [delta_hi, delta_hi, delta - delta_hi, jnp.zeros((104, 512), F32)], axis=0
         ).astype(BF)
-
-        @pl.loop(0, 4)
-        def _(k, half=half, zz=zz, spread=spread, weight=weight):
+        return zz, spread, weight
+
+    def product(half, first, last, found):
+        zz, spread, weight = found
+
+        @pl.loop(first, last)
+        def _(k):
             at = chunk(chunk_at(k))
-
-            @pl.when(k >= 2)
-            def _():
-                join(half, k - 2)
-
             if half == 0:
                 for p in range(4):
                     arrive(alpha_slot(k, p, 1 - c), c_recv.at[k, p])
                 total = jnp.dot(alpha[at, :], pick[...], preferred_element_type=F32)
                 total_hi = total.astype(BF).astype(F32)
                 sums[at, :] = jnp.where(low_lanes, total - total_hi, total_hi).astype(BF)
-            block = jnp.dot(alpha[at, :], beta[zz], preferred_element_type=F32)
+            block = jnp.dot(alpha[at, :], beta[zz].reshape(8 * TOK, 512), preferred_element_type=F32)
             block = block + jnp.dot(sums[at, :], spread, preferred_element_type=F32)
             block = block * weight
             partial[half, at, :] = block.astype(BF)
-
-            @pl.when(k < 2)
-            def _():
+            if first < 2:
                 exact[k] = block
 
                 @pl.when(outer)
                 def _():
-                    hand(half, k).start()
-
-                if half == 0:
-                    relay_alpha(k + 2)
-
-                    @pl.when(k == 1)
-                    def _():
-                        relay_x(1)
-
-            @pl.when(k == 2)
-            def _():
-                deliver_all(half, 2)
-
-        @pl.loop(1, 8)
-        def _(j, half=half):
-            deliver(half, 3, lax.rem(me + j, 8)).start()
-
-        landed[half, 0, me] = partial[half, pl.ds(pl.multiple_of(s * 32, 32), 32), :]
+                    for part in range(2):
+                        hand(half, k, part).start()
+
+            else:
+
+                @pl.when(k == 2)
+                def _():
+                    deliver_all(half, 2)
+
+        if last == 4:
+
+            @pl.loop(1, 8)
+            def _(j):
+                deliver(half, 3, lax.rem(me + j, 8)).start()
+
+            landed[half, 0, me] = partial[half, pl.ds(pl.multiple_of(s * 32, 32), 32), :]
+
+    found = columns_in(0)
+    product(0, 0, 2, found)
+    far_in(1)
+    mine = panel.at[1 - zh, x]
+    arrive(mine, p_recv.at[1, x])
+    for i, p in enumerate(x_peers):
+        go(mine, mine, p_send.at[3 + i], p_recv.at[2, x], (p * 2 + zh, s))
+    relay_alpha(3)
+    relay_x(1, 0)
+    product(0, 2, 4, found)
+    join(0, 0)
+    relay_x(1, 1)
+    join(0, 1)
+    found = columns_in(1)
+    product(1, 0, 2, found)
+    product(1, 2, 4, found)
+    join(1, 0)
+    join(1, 1)
 
     for half in range(2):
         zz = zh if half == 0 else 1 - zh
@@ -502,19 +534,23 @@
         @pl.when(outer)
         def _(half=half):
             for k in range(2):
-                hand(half, k).wait_send()
+                for part in range(2):
+                    hand(half, k, part).wait_send()
 
     @pl.loop(1, 8)
     def _(i):
         q = lax.rem(me + i, 8)
-        share(0, q).wait_send()
-        share(1, q).wait_send()
-
-    for k in range(4):
-        over_z(k).wait_send()
+        share_near(q).wait_send()
+        for part in range(2):
+            share_far(part, q).wait_send()
+
+    for part in range(2):
+        for k in range(4):
+            over_z(part, k).wait_send()
     for far in range(2):
         for part in range(2):
-            pass_on(far, part).wait_send()
+            for i in range(2):
+                pass_on(far, part, i).wait_send()
     for ck in range(2):
         to_sibling(ck).wait_send()
     for k in range(4):
@@ -542,26 +578,26 @@
             pltpu.VMEM((2, 2, 4, 4, 32, TAPS), F32),
             pltpu.VMEM((CHAN, TOK), F32),
             pltpu.VMEM((CHAN, TOK), BF),
-            pltpu.VMEM((8, TOK, 128), BF),
-            pltpu.VMEM((8, TOK, 128), BF),
+            pltpu.VMEM((2, 8, 128, 128), BF),
+            pltpu.VMEM((2, 8, 128, 128), BF),
             pltpu.VMEM((2, 2, 8, 128), F32),
-            pltpu.VMEM((8, 2, 2, 8, 128), F32),
             pltpu.VMEM((4, 2, 2, 8, 128), F32),
+            pltpu.VMEM((8, 2, 3, 8, 128), F32),
             pltpu.VMEM((2, 2, 8, 128), F32),
             pltpu.VMEM((2, 4, 16, 128), F32),
             pltpu.VMEM((8 * TOK, 128), BF),
             pltpu.VMEM((CHAN, 128), BF),
             pltpu.VMEM((CHAN, 8 * TOK), BF),
-            pltpu.VMEM((2, 8 * TOK, 512), BF),
+            pltpu.VMEM((2, 8, 2, 128, 512), BF),
             pltpu.VMEM((2, CHAN, 512), BF),
             pltpu.VMEM((2, CHUNK, 512), F32),
             pltpu.VMEM((2, 2, CHUNK, 512), BF),
             pltpu.VMEM((2, 3, 8, 32, 512), BF),
             DMA((2,)), DMA((2,)), DMA((2, 3)), DMA((2, 4)), DMA((2, 3)), DMA((2, 4)), DMA((2,)), DMA((2,)),
-            DMA((8,)), DMA((8,)), DMA((3,)), DMA((4,)),
-            DMA((8,)), DMA((8,)), DMA((8,)), DMA((8,)), DMA((4, 3)), DMA((4, 4)), DMA((4, 4)), DMA((4, 4)),
-            DMA((4,)), DMA((4,)), DMA((2, 3, 2)), DMA((2, 3, 2)), DMA((7,)), DMA((3, 4)), DMA((2, 2)), DMA((2, 2)),
-            DMA((2, 4, 8)), DMA((2, 3, 8)), DMA((2,)), DMA((2, 2)),
+            DMA((2, 3)), DMA((2, 4)), DMA((2, 8)), DMA((2, 8)),
+            DMA((8,)), DMA((8,)), DMA((2, 8)), DMA((2, 8)), DMA((4, 3)), DMA((4, 4)), DMA((4, 4)), DMA((4, 4)),
+            DMA((2, 4)), DMA((2, 4)), DMA((2, 2, 2, 2)), DMA((2, 3, 2, 2)), DMA((7,)), DMA((3, 4)),
+            DMA((2, 2, 2)), DMA((2, 2, 2)), DMA((2, 4, 8)), DMA((2, 3, 8)), DMA((2,)), DMA((2, 2)),
         ],
         compiler_params=pltpu.CompilerParams(
             collective_id=0, has_side_effects=True, vmem_limit_bytes=56 * 2**20

time: 128 us -> 116 us (0.906)
  the two profiles are of different devices: /device:TPU:161 before, /device:TPU:41 now
where the time goes in v3:
time: 116 us; the launch traced here: 115 us
  Pallas kernels  112 us (97%)
  local copies, waits for them, and re-layouts  2.26 us (2%)
    pallas_call x1, Pallas kernels, body(): pl.pallas_call(kernel, out_shape=jax.ShapeDtypeStruct((32, 8 * CHAN), F32...  112 us

profile of v3, /device:TPU:41, one launch (start us, length us, event | category | flops | bytes accessed | tf_op | source)
XLA Modules:
  0.0 114.6 jit_solution(15829832321265999853)
XLA Ops:
  0.0 112.4 %correlate.1 = f32[32,8192]{1,0:T(8,128)} custom-call(bf16[3,1024,256]{2,1,0:T(8,128)(2,1)} %all_a.1, bf16[3,1024,256]{2,1,0:T(8,128)(2,1)} %all_b.1, f32[32,128]{1,0:T(8,128)} %filt_a.1, f32[32,128]{1,0:T(8,128)} %filt_b.1, bf16[256,256]{1,0:T(8,128)(2,1)} %constant.8.clone.wf_hi, bf16[256,256]{1,0:T(8,128)(2,1)} %constant.9.clone.wf_lo, ...), custom_call_target="tpu_custom_call" | custom-call | tf_op jit(solution)/shard_map/correlate/pallas_call | solution.py:569
  112.4 2.3 %copy.10 = f32[32,8192]{1,0:T(8,128)} copy(f32[32,8192]{1,0:T(8,128)} %correlate.1) | data formatting | bytes 2097152

commit v4 on v3

--- a/solution.py
+++ b/solution.py
@@ -155,19 +155,16 @@
         for i, p in enumerate(zl_peers):
             mine = taps.at[ck, c, y, zl]
             go(mine, mine, f1_send.at[ck, i], f1_recv.at[ck, zl], seq(p, y, c))
-    for ck in range(2):
-        halo_out(ck)
+    halo_out(0)
     for ck in range(2):
         for p in zl_peers:
             arrive(taps.at[ck, c, y, p], f1_recv.at[ck, p])
-        first = [taps_copy(ck, i, p) for i, p in enumerate(y_peers)]
-        for cp in first:
+        for i, p in enumerate(y_peers):
+            cp = taps_copy(ck, i, p)
             cp.start()
+            sends.append(cp)
         if ck == 0:
-            for cp in first:
-                cp.wait_send()
-        else:
-            sends.extend(first)
+            halo_out(1)
 
     lane = lax.broadcasted_iota(jnp.int32, (8 * TOK, 128), 1)
     slot = lax.broadcasted_iota(jnp.int32, (8 * TOK, 128), 0) // TOK
@@ -303,8 +300,11 @@
     def _(i):
         centred[chunk(i), :] = convolve(0, rows_a, i)
 
+        @pl.when(i == 2)
+        def _():
+            filters_half(1)
+
     level_z(0)
-    filters_half(1)
     level_y(0)
 
     filters_rest(1)
@@ -342,9 +342,9 @@
             shift_c = to_column(shifts[0, 0, pl.ds(block, 1), :], eye)
             scale_c = to_column(shifts[0, 1, pl.ds(block, 1), :], eye)
             z_a[channels(block), :] = ((centred[channels(block), :] + shift_c) * scale_c).astype(BF)
-    level_y(1)
     for k in range(4):
         over_z(0, k).start()
+    level_y(1)
     alpha_out(0)
     alpha_out(1)
     keep_a = pltpu.make_async_copy(z_a, alpha.at[:, columns(me)], local.at[1])
@@ -356,7 +356,6 @@
         arrive(beta.at[zh, q, :, :, channels(x)], y_recv.at[q])
     for part in range(2):
         spread_x(0, part)
-    alpha_out(2)
     relay_x(0, 0)
     for k in range(4):
         over_z(1, k).start()
@@ -391,12 +390,13 @@
         spread_x(1, part)
 
     relay_z(0)
-    alpha_out(3)
+    alpha_out(2)
     relay_x(0, 1)
     far_in(0)
     relay_alpha(0)
     relay_alpha(1)
     relay_z(1)
+    alpha_out(3)
     relay_alpha(2)
     keep_a.wait()
 
@@ -492,12 +492,13 @@
     arrive(mine, p_recv.at[1, x])
     for i, p in enumerate(x_peers):
         go(mine, mine, p_send.at[3 + i], p_recv.at[2, x], (p * 2 + zh, s))
+    relay_x(1, 0)
+    product(0, 2, 3, found)
+    join(0, 0)
     relay_alpha(3)
-    relay_x(1, 0)
-    product(0, 2, 4, found)
-    join(0, 0)
     relay_x(1, 1)
     join(0, 1)
+    product(0, 3, 4, found)
     found = columns_in(1)
     product(1, 0, 2, found)
     product(1, 2, 4, found)

time: 116 us -> 113 us (0.974); the launches traced: 115 us -> 113 us
    pallas_call x1, Pallas kernels: 112 us -> 111 us  [body(): pl.pallas_call(kernel, out_shape=jax.ShapeDtypeStruct((32, 8 * CHAN), F32...]
where the time goes in v4:
time: 113 us
  Pallas kernels  111 us (98%)
  local copies, waits for them, and re-layouts  2.26 us (2%)
    pallas_call x1, Pallas kernels, body(): pl.pallas_call(kernel, out_shape=jax.ShapeDtypeStruct((32, 8 * CHAN), F32...  111 us
    unnamed x1, local copies, waits for them, and re-layouts  2.26 us

profile of v4, /device:TPU:41, one launch (start us, length us, event | category | flops | bytes accessed | tf_op | source)
XLA Modules:
  0.0 113.1 jit_solution(6476518457472846345)
XLA Ops:
  0.0 110.8 %correlate.1 = f32[32,8192]{1,0:T(8,128)} custom-call(bf16[3,1024,256]{2,1,0:T(8,128)(2,1)} %all_a.1, bf16[3,1024,256]{2,1,0:T(8,128)(2,1)} %all_b.1, f32[32,128]{1,0:T(8,128)} %filt_a.1, f32[32,128]{1,0:T(8,128)} %filt_b.1, bf16[256,256]{1,0:T(8,128)(2,1)} %constant.8.clone.wf_hi, bf16[256,256]{1,0:T(8,128)(2,1)} %constant.9.clone.wf_lo, ...), custom_call_target="tpu_custom_call" | custom-call | tf_op jit(solution)/shard_map/correlate/pallas_call | solution.py:570
  110.8 2.3 %copy.10 = f32[32,8192]{1,0:T(8,128)} copy(f32[32,8192]{1,0:T(8,128)} %correlate.1) | data formatting | bytes 2097152

commit v5 on v4

--- a/solution.py
+++ b/solution.py
@@ -69,10 +69,10 @@
 def kernel(
     all_a, all_b, filt_a, filt_b, wf_hi, wf_lo, wi_hi, wi_lo, out,
     kept, edge, halo, taps, centred, z_a, z_b, across, own, level1, level2, shifts, panel, pick, sums, alpha, beta,
-    partial, exact, passed, landed,
+    partial, exact, passed, landed, result,
     h_send, h_recv, f1_send, f1_recv, f2_send, f2_recv, f3_send, f3_recv, s1_send, s1_recv, s2_send, s2_recv,
     y_send, y_recv, w_send, w_recv, a_send, a_recv, c_send, c_recv, z_send, z_recv, x_send, x_recv, p_send, p_recv, r_send, r_recv, o_send, o_recv,
-    local, l_sem,
+    local, l_sem, done,
 ):
     g, s, x, zh, zl, y, c = place()
     me = y * 2 + c
@@ -505,6 +505,7 @@
     join(1, 0)
     join(1, 1)
 
+    writes = []
     for half in range(2):
         zz = zh if half == 0 else 1 - zh
 
@@ -521,7 +522,13 @@
             total = total + landed[half, 2, q].astype(F32)
             for p in range(4):
                 at = pl.multiple_of((p * 2 + zz) * 1024 + q * 128, 128)
-                out[:, pl.ds(at, 128)] = total[:, p * 128 : (p + 1) * 128]
+                result[:, pl.ds(at, 128)] = total[:, p * 128 : (p + 1) * 128]
+
+        for p in range(4):
+            at = pl.ds(pl.multiple_of((p * 2 + zz) * 1024, 1024), 1024)
+            write = pltpu.make_async_copy(result.at[:, at], out.at[:, at], done.at[half, p])
+            write.start()
+            writes.append(write)
 
     for half in range(2):
         for k in range(4):
@@ -559,6 +566,8 @@
             alpha_copy(k, p).wait_send()
     for cp in sends:
         cp.wait_send()
+    for write in writes:
+        write.wait()
 
 
 VMEM = pl.BlockSpec(memory_space=pltpu.VMEM)
@@ -571,7 +580,7 @@
         kernel,
         out_shape=jax.ShapeDtypeStruct((32, 8 * CHAN), F32),
         in_specs=[pl.BlockSpec(memory_space=pl.ANY)] * 2 + [VMEM] * 6,
-        out_specs=VMEM,
+        out_specs=pl.BlockSpec(memory_space=pl.ANY),
         scratch_shapes=[
             pltpu.VMEM((2, 3, CHAN, TOK), BF),
             pltpu.VMEM((2, CHAN, 128), BF),
@@ -594,11 +603,12 @@
             pltpu.VMEM((2, CHUNK, 512), F32),
             pltpu.VMEM((2, 2, CHUNK, 512), BF),
             pltpu.VMEM((2, 3, 8, 32, 512), BF),
+            pltpu.VMEM((32, 8 * CHAN), F32),
             DMA((2,)), DMA((2,)), DMA((2, 3)), DMA((2, 4)), DMA((2, 3)), DMA((2, 4)), DMA((2,)), DMA((2,)),
             DMA((2, 3)), DMA((2, 4)), DMA((2, 8)), DMA((2, 8)),
             DMA((8,)), DMA((8,)), DMA((2, 8)), DMA((2, 8)), DMA((4, 3)), DMA((4, 4)), DMA((4, 4)), DMA((4, 4)),
             DMA((2, 4)), DMA((2, 4)), DMA((2, 2, 2, 2)), DMA((2, 3, 2, 2)), DMA((7,)), DMA((3, 4)),
-            DMA((2, 2, 2)), DMA((2, 2, 2)), DMA((2, 4, 8)), DMA((2, 3, 8)), DMA((2,)), DMA((2, 2)),
+            DMA((2, 2, 2)), DMA((2, 2, 2)), DMA((2, 4, 8)), DMA((2, 3, 8)), DMA((2,)), DMA((2, 2)), DMA((2, 4)),
         ],
         compiler_params=pltpu.CompilerParams(
             collective_id=0, has_side_effects=True, vmem_limit_bytes=56 * 2**20

time: 113 us -> 112 us (level)
  no operation moved by 1% of the time
where the time goes in v5:
time: 112 us
  Pallas kernels  110 us (98%)
  local copies, waits for them, and re-layouts  2.26 us (2%)
    pallas_call x1, Pallas kernels, body(): pl.pallas_call(kernel, out_shape=jax.ShapeDtypeStruct((32, 8 * CHAN), F32...  110 us
    unnamed x1, local copies, waits for them, and re-layouts  2.26 us

profile of v5, /device:TPU:41, one launch (start us, length us, event | category | flops | bytes accessed | tf_op | source)
XLA Modules:
  0.0 112.2 jit_solution(3843026903786426682)
XLA Ops:
  0.0 109.9 %correlate.1 = f32[32,8192]{1,0:T(8,128)} custom-call(bf16[3,1024,256]{2,1,0:T(8,128)(2,1)} %all_a.1, bf16[3,1024,256]{2,1,0:T(8,128)(2,1)} %all_b.1, f32[32,128]{1,0:T(8,128)} %filt_a.1, f32[32,128]{1,0:T(8,128)} %filt_b.1, bf16[256,256]{1,0:T(8,128)(2,1)} %constant.8.clone.wf_hi, bf16[256,256]{1,0:T(8,128)(2,1)} %constant.9.clone.wf_lo, ...), custom_call_target="tpu_custom_call" | custom-call | tf_op jit(solution)/shard_map/correlate/pallas_call | solution.py:579
  109.9 2.3 %copy.10 = f32[32,8192]{1,0:T(8,128)} copy(f32[32,8192]{1,0:T(8,128)} %correlate.1) | data formatting | bytes 2097152
